TPU v7x, 256 devices: a whole 4x4x8 slice. The times are simulated.
256 devices in a mesh: row: 16 (over z, core), grid: 16 (over x, y).
Axes of the slice: x: 4, y: 4, z: 8, core: 2. Of those that a mesh axis runs over, the one named last changes fastest.
Arguments:
- right_side: float32 [64, 32, 192, 256], P('row', 'grid'), may hold values from -6 to 6
- fine_blocks: bfloat16 [64, 32, 6, 192, 192], P('row', 'grid')
- fine_columns: int32 [64, 32, 6], P('row', 'grid'), may hold values from 0 to 8, as said below
- fine_prolong: bfloat16 [64, 32, 2, 192, 192], P('row', 'grid'), may hold values from -0.21875 to 0.21875
- fine_targets: int32 [64, 32, 2], P('row', 'grid'), may hold values from 0 to 7
- middle_blocks: bfloat16 [128, 3, 192, 192], P('row')
- middle_columns: int32 [128, 3], P('row'), may hold values from 0 to 2, as said below
- middle_prolong: bfloat16 [128, 2, 192, 192], P('row'), may hold values from -0.21875 to 0.21875
- middle_targets: int32 [128, 2], P('row'), may hold values from 0 to 3
Outputs:
- smooth_fine: float32 [64, 32, 192, 256], P('row', 'grid')
- smooth_middle: float32 [128, 192, 256], P('row')
- coarsest_right: float32 [4, 192, 256], replicated
Inputs may be any that keep to these rules, and one draw needn't show every extreme that they name: `fine_columns`: slot 0 of every block row is 4, its own block; entries of other slots may repeat. `middle_columns`: slot 0 of every block row is 1, its own block. In each aligned group of 8 block rows, slot 1 of the first row is 0 and slot 2 of the last row is 2; entries of other slots may repeat.
All inputs are finite; a program needn't handle non-finite values.
Results may differ from a plain program's by a relative error of at most 0.033.
Values may be sent and summed in bfloat16 or wider, within the bound.
A program may use at most 128 MiB of HBM per device.

v0:
```python
from functools import partial

import jax
import jax.numpy as jnp
from jax import lax
from jax.sharding import PartitionSpec as P

C3 = 4
DEG = 3


cheb_low = 0.6
cheb_high = 6.0


def padded(cells, sides, width):
    for axis, dim in sides:
        count = lax.axis_size(axis)
        ends = count - 1
        head = lax.slice_in_dim(cells, 0, width, axis=dim)
        tail = lax.slice_in_dim(cells, cells.shape[dim] - width, cells.shape[dim], axis=dim)
        cells = jnp.concatenate(
            [
                lax.ppermute(tail, axis, [(i, (i + 1) % count) for i in range(ends)]),
                cells,
                lax.ppermute(head, axis, [((i + 1) % count, i) for i in range(ends)]),
            ],
            axis=dim,
        )
    return cells


def chebyshev(apply_operator, right_part):
    central_value = 0.5 * (cheb_high + cheb_low)
    half_width = 0.5 * (cheb_high - cheb_low)
    ratio_value = central_value / half_width
    rho_old = 1.0 / ratio_value
    direction = right_part / central_value
    iterate = direction
    residual = right_part
    for sweep_index in range(DEG):
        residual = residual - apply_operator(direction.astype(jnp.bfloat16))
        if sweep_index + 1 < DEG:
            rho_new = 1.0 / (2.0 * ratio_value - rho_old)
            direction = rho_new * rho_old * direction + 2.0 * rho_new / half_width * residual
            iterate = iterate + direction
            rho_old = rho_new
    return (iterate, residual)


def fine_product(block_matrices, columns, vector):
    padded_input = padded(vector, (("row", 0), ("grid", 1)), 1)
    rows_first = vector.shape[0]
    row_width = vector.shape[1] + 2
    flattened = padded_input.reshape((rows_first + 2) * row_width, vector.shape[2], vector.shape[3])
    offset_rows = lax.broadcasted_iota(jnp.int32, columns.shape, 0)
    offset_cols = lax.broadcasted_iota(jnp.int32, columns.shape, 1)
    position = (offset_rows + columns // 3) * row_width + offset_cols + columns % 3
    picked = jnp.take(flattened, position.reshape(-1), axis=0).reshape(
        columns.shape + flattened.shape[1:]
    )
    return jnp.einsum(
        "xykab,xykbn->xyan", block_matrices, picked, preferred_element_type=jnp.float32
    )


def middle_product(block_matrices, columns, vector):
    padded_input = padded(vector, (("row", 0),), 1)
    position = lax.broadcasted_iota(jnp.int32, columns.shape, 0) + columns
    picked = jnp.take(padded_input, position.reshape(-1), axis=0).reshape(
        columns.shape + padded_input.shape[1:]
    )
    return jnp.einsum("ikab,ikbn->ian", block_matrices, picked, preferred_element_type=jnp.float32)


def scatter_blocks(pieces, targets, count):
    flattened_parts = pieces.reshape((-1,) + pieces.shape[-2:])
    flat_targets = targets.reshape(-1)
    owning_rows = lax.broadcasted_iota(jnp.int32, (flat_targets.shape[0], count), 1)
    selection_mask = (flat_targets[:, None] == owning_rows).astype(jnp.float32)
    return jnp.einsum(
        "oz,oay->zay", selection_mask, flattened_parts, precision=lax.Precision.HIGHEST
    )


def middle_level(block_matrices, columns, prolongation, targets, right_part):
    iterate, residual = chebyshev(partial(middle_product, block_matrices, columns), right_part)
    pieces = jnp.einsum(
        "ikab,ian->ikbn",
        prolongation,
        residual.astype(jnp.bfloat16),
        preferred_element_type=jnp.float32,
    )
    local_total = scatter_blocks(pieces, targets, C3)
    return (iterate, lax.psum(local_total.astype(jnp.bfloat16), "row").astype(jnp.float32))


def body(
    right_side,
    fine_blocks,
    fine_columns,
    fine_prolong,
    fine_targets,
    middle_blocks,
    middle_columns,
    middle_prolong,
    middle_targets,
):
    smooth_fine, fine_residual = chebyshev(
        partial(fine_product, fine_blocks, fine_columns), right_side
    )
    pieces = jnp.einsum(
        "xykab,xyan->xykbn",
        fine_prolong,
        fine_residual.astype(jnp.bfloat16),
        preferred_element_type=jnp.float32,
    )
    partial_sum = scatter_blocks(pieces, fine_targets, middle_blocks.shape[0])
    middle_right = lax.psum(partial_sum.astype(jnp.bfloat16), "grid").astype(jnp.float32)
    smooth_middle, coarsest_right = middle_level(
        middle_blocks, middle_columns, middle_prolong, middle_targets, middle_right
    )
    return (smooth_fine, smooth_middle, coarsest_right)


def solution(mesh):
    placed = (
        P("row", "grid", None, None),
        P("row", "grid", None, None, None),
        P("row", "grid", None),
        P("row", "grid", None, None, None),
        P("row", "grid", None),
        P("row", None, None, None),
        P("row", None),
        P("row", None, None, None),
        P("row", None),
    )
    return jax.shard_map(
        body,
        mesh=mesh,
        in_specs=placed,
        out_specs=(P("row", "grid", None, None), P("row", None, None), P()),
        check_vma=False,
    )
```

profile of v0, /device:TPU:1, one launch (start us, length us, event | category | flops | bytes accessed | tf_op | source)
XLA Modules:
  0.0 445.8 jit_solution(12434600352052097026)
XLA Ops:
  7.2 1.7 multiply_convert_fusion
  9.0 5.1 %collective-permute-start.1 = (bf16[1,2,192,256]{3,2,1,0:T(8,128)(2,1)S(1)}, bf16[1,2,192,256]{3,2,1,0:T(8,128)(2,1)S(1)}, u32[]{:S(2)}, u32[]{:S(2)}) collective-permute-start(bf16[1,2,192,256]{3,2,1,0:T(8,128)(2,1)S(1)} %get-tuple-element.34), channel_id=1, source_target_pairs={{16,0},{32,16},{48,32},{64,48},{80,64},{96,80},{112,96},{128,112},... | collective-permute-start | bytes 589832 | tf_op jit(solution)/shard_map/ppermute | solution.py:26
  14.2 1.9 collective-permute-start
  16.1 1.2 collective-permute-done.1
  17.3 1.4 collective-permute-done
  19.9 1.3 collective-permute-start.3
  21.2 4.8 %collective-permute-start.2 = (bf16[6,1,192,256]{3,2,1,0:T(8,128)(2,1)}, bf16[6,1,192,256]{3,2,1,0:T(8,128)(2,1)}, u32[]{:S(2)}, u32[]{:S(2)}) collective-permute-start(bf16[6,1,192,256]{3,2,1,0:T(8,128)(2,1)} %get-tuple-element.21), channel_id=1, source_target_pairs={{0,1},{1,2},{2,3},{3,4},{4,5},{5,6},{6,7},{7,8},{8,9},{9,10},{10,1... | collective-permute-start | bytes 1769480 | tf_op jit(solution)/shard_map/ppermute | solution.py:24
  26.2 10.4 %collective-permute-done.3 = bf16[6,1,192,256]{3,2,1,0:T(8,128)(2,1)} collective-permute-done((bf16[6,1,192,256]{3,2,1,0:T(8,128)(2,1)}, bf16[6,1,192,256]{3,2,1,0:T(8,128)(2,1)}, u32[]{:S(2)}, u32[]{:S(2)}) %collective-permute-start.3) | collective-permute-done | bytes 589856 | tf_op jit(solution)/shard_map/ppermute | solution.py:26
  36.6 1.8 collective-permute-done.2
  38.3 2.6 pad_maximum_fusion
  41.0 4.9 %gather_fusion = bf16[48,192,256]{2,1,0:T(8,128)(2,1)} fusion(bf16[24,192,256]{2,1,0:T(8,128)(2,1)} %bitcast.97, s32[1024]{0:T(1024)S(1)} %pad_clamp_fusion.1), kind=kCustom, calls=%fused_computation.clone | custom fusion | bytes 9437376 | tf_op jit(solution)/shard_map/jit(_take)/gather | solution.py:59
  45.9 3.0 broadcast_select_fusion.2
  50.0 2.6 fusion.22
  52.6 2.0 collective-permute-start.5
  54.6 3.8 collective-permute-start.4
  58.4 1.4 collective-permute-done.5
  61.3 1.3 collective-permute-start.7
  62.6 4.8 %collective-permute-start.6 = (bf16[6,1,192,256]{3,2,1,0:T(8,128)(2,1)S(1)}, bf16[6,1,192,256]{3,2,1,0:T(8,128)(2,1)S(1)}, u32[]{:S(2)}, u32[]{:S(2)}) collective-permute-start(bf16[6,1,192,256]{3,2,1,0:T(8,128)(2,1)S(1)} %get-tuple-element.19), channel_id=1, source_target_pairs={{0,1},{1,2},{2,3},{3,4},{4,5},{5,6},{6,7},{7,8},{8,9},{9,10},{10,1... | collective-permute-start | bytes 1769480 | tf_op jit(solution)/shard_map/ppermute | solution.py:24
  67.3 8.8 %collective-permute-done.7 = bf16[6,1,192,256]{3,2,1,0:T(8,128)(2,1)S(1)} collective-permute-done((bf16[6,1,192,256]{3,2,1,0:T(8,128)(2,1)S(1)}, bf16[6,1,192,256]{3,2,1,0:T(8,128)(2,1)S(1)}, u32[]{:S(2)}, u32[]{:S(2)}) %collective-permute-start.7) | collective-permute-done | bytes 589856 | tf_op jit(solution)/shard_map/ppermute | solution.py:26
  76.2 1.8 collective-permute-done.6
  77.9 1.6 pad_maximum_fusion.1
  79.5 4.9 %gather_fusion.1 = bf16[48,192,256]{2,1,0:T(8,128)(2,1)} fusion(bf16[24,192,256]{2,1,0:T(8,128)(2,1)} %bitcast.98, s32[1024]{0:T(1024)S(1)} %pad_clamp_fusion.1), kind=kCustom, calls=%fused_computation.2.clone | custom fusion | bytes 9437376 | tf_op jit(solution)/shard_map/jit(_take)/gather | solution.py:59
  84.5 3.0 broadcast_select_fusion.1
  87.5 1.5 slice-done.3
  89.0 3.3 fusion.20
  92.4 1.9 collective-permute-start.9
  94.3 6.3 %collective-permute-start.8 = (bf16[1,2,192,256]{3,2,1,0:T(8,128)(2,1)S(1)}, bf16[1,2,192,256]{3,2,1,0:T(8,128)(2,1)S(1)}, u32[]{:S(2)}, u32[]{:S(2)}) collective-permute-start(bf16[1,2,192,256]{3,2,1,0:T(8,128)(2,1)S(1)} %get-tuple-element.29), channel_id=1, source_target_pairs={{0,16},{16,32},{32,48},{48,64},{64,80},{80,96},{96,112},{112,128},... | collective-permute-start | bytes 589832 | tf_op jit(solution)/shard_map/ppermute | solution.py:24
  100.7 1.4 collective-permute-done.9
  104.5 1.4 collective-permute-start.11
  105.9 5.6 %collective-permute-start.10 = (bf16[6,1,192,256]{3,2,1,0:T(8,128)(2,1)}, bf16[6,1,192,256]{3,2,1,0:T(8,128)(2,1)}, u32[]{:S(2)}, u32[]{:S(2)}) collective-permute-start(bf16[6,1,192,256]{3,2,1,0:T(8,128)(2,1)} %get-tuple-element.17), channel_id=1, source_target_pairs={{0,1},{1,2},{2,3},{3,4},{4,5},{5,6},{6,7},{7,8},{8,9},{9,10},{10,1... | collective-permute-start | bytes 1769480 | tf_op jit(solution)/shard_map/ppermute | solution.py:24
  111.5 2.7 copy.27
  114.4 2.7 collective-permute-done.11
  117.0 1.8 collective-permute-done.10
  118.8 2.6 pad_maximum_fusion.2
  121.4 4.9 %gather_fusion.2 = bf16[48,192,256]{2,1,0:T(8,128)(2,1)} fusion(bf16[24,192,256]{2,1,0:T(8,128)(2,1)} %bitcast.96, s32[1024]{0:T(1024)S(1)} %pad_clamp_fusion.1), kind=kCustom, calls=%fused_computation.3.clone | custom fusion | bytes 9437376 | tf_op jit(solution)/shard_map/jit(_take)/gather | solution.py:59
  126.3 5.0 %broadcast_select_fusion = bf16[48,192,256]{2,1,0:T(8,128)(2,1)} fusion(bf16[48,192,256]{2,1,0:T(8,128)(2,1)} %gather_fusion.2, pred[48]{0:T(512)(128)(4,1)S(1)} %compare_and_fusion.1), kind=kLoop, calls=%fused_computation.6 | loop fusion | flops 2359296 | bytes 9437232 | tf_op jit(solution)/shard_map/jit(_take)/select_n | solution.py:59
  131.4 8.0 %fusion.10 = f32[4,2,256,384]{2,3,1,0} fusion(bf16[4,2,192,384]{2,3,1,0:T(8,128)(2,1)} %bitcast.108, f32[4,2,192,256]{3,2,1,0:T(8,128)} %get-tuple-element.37, bf16[4,2,6,192,192]{4,3,2,1,0:T(8,128)(2,1)} %param.14, bf16[4,2,6,192,256]{4,3,2,1,0:T(8,128)(2,1)} %bitcast.101), kind=kOutput, calls=%fused_computation.43 | convolution fusion | flops 1208745984 | bytes 14155776
  139.4 5.6 %fusion.11 = bf16[8,192,256]{2,0,1:T(8,128)(2,1)} fusion(f32[16,192,256]{2,1,0:T(8,128)} %bitcast.106, s32[16]{0:T(128)S(1)} %eq.24), kind=kOutput, calls=%fused_computation.44 | convolution fusion | flops 75890816 | bytes 3932224 | tf_op jit(solution)/shard_map/oz,oay->zay/dot_general | solution.py:81
  145.2 109.3 %all-reduce.3.cloned.1.call-done = bf16[8,192,256]{2,0,1:T(8,128)(2,1)} async-done(((bf16[8,192,256]{2,0,1:T(8,128)(2,1)}), bf16[8,192,256]{2,0,1:T(8,128)(2,1)}) %all-reduce.3.cloned.1.call-update) | async-done | bytes 786448 | tf_op jit(solution)/shard_map/psum | solution.py:119
  254.5 1.3 fusion.5
  256.1 3.9 collective-permute-start.13
  260.0 3.1 collective-permute-start.12
  263.1 1.4 collective-permute-done.13
  267.0 2.2 gather_fusion.3
  269.2 2.0 broadcast_select_fusion.5
  273.7 1.9 collective-permute-start.15
  275.6 4.6 %collective-permute-start.14 = (bf16[1,192,256]{2,0,1:T(2,128)(2,1)S(1)}, bf16[1,192,256]{2,0,1:T(2,128)(2,1)S(1)}, u32[]{:S(2)}, u32[]{:S(2)}) collective-permute-start(bf16[1,192,256]{2,0,1:T(2,128)(2,1)S(1)} %get-tuple-element.25), channel_id=1, source_target_pairs={{0,16},{16,32},{32,48},{48,64},{64,80},{80,96},{96,112},{112,128},... | collective-permute-start | bytes 294920 | tf_op jit(solution)/shard_map/ppermute | solution.py:24
  280.2 1.2 collective-permute-done.15
  283.6 1.3 copy.32
  284.9 3.4 gather_fusion.4
  288.3 2.0 broadcast_select_fusion.4
  291.7 3.4 fusion.14
  296.2 1.9 collective-permute-start.17
  298.2 4.4 collective-permute-start.16
  302.6 2.7 copy.37
  305.5 2.3 pad_maximum_fusion.5
  307.8 1.3 copy.35
  309.1 3.4 gather_fusion.5
  312.5 2.0 broadcast_select_fusion.3
  316.3 3.4 fusion.8
  320.3 3.8 fusion.15
  324.1 3.1 copy.39
  327.2 109.8 %all-reduce.5.cloned.1.call-done = bf16[4,192,256]{2,0,1:T(4,128)(2,1)} async-done(((bf16[4,192,256]{2,0,1:T(4,128)(2,1)}), bf16[4,192,256]{2,0,1:T(4,128)(2,1)}) %all-reduce.5.cloned.1.call-update) | async-done | bytes 393232 | tf_op jit(solution)/shard_map/psum | solution.py:95
  437.0 1.9 copy.40
  (88 shorter events, 19.4 us)
Async XLA Ops:
  7.2 264.0 %copy-start = (bf16[8,3,192,192]{3,2,1,0:T(8,128)(2,1)S(1)}, bf16[8,3,192,192]{3,2,1,0:T(8,128)(2,1)}, u32[]{:S(2)}) copy-start(bf16[8,3,192,192]{3,2,1,0:T(8,128)(2,1)} %param.18) | copy-start | bytes 5308420
  7.2 247.3 %all-reduce.3.cloned.1.call-start = ((), (), s32[]{:S(2)}) async-start(), calls=%async_computation | async-start | bytes 1572864 | tf_op jit(solution)/shard_map/psum | solution.py:119
  9.0 8.3 %collective-permute-start.1 = (bf16[1,2,192,256]{3,2,1,0:T(8,128)(2,1)S(1)}, bf16[1,2,192,256]{3,2,1,0:T(8,128)(2,1)S(1)}, u32[]{:S(2)}, u32[]{:S(2)}) collective-permute-start(bf16[1,2,192,256]{3,2,1,0:T(8,128)(2,1)S(1)} %get-tuple-element.34), channel_id=1, source_target_pairs={{16,0},{32,16},{48,32},{64,48},{80,64},{96,80},{112,96},{128,112},... | collective-permute-start | bytes 589832 | tf_op jit(solution)/shard_map/ppermute | solution.py:26
  14.1 11.9 %copy-start.13 = (s32[4,2,6]{2,1,0:T(2,128)S(1)}, s32[4,2,6]{2,1,0:T(2,128)}, u32[]{:S(2)}) copy-start(s32[4,2,6]{2,1,0:T(2,128)} %param.15) | copy-start | bytes 580
  14.2 4.5 %collective-permute-start = (bf16[1,2,192,256]{3,2,1,0:T(8,128)(2,1)S(1)}, bf16[1,2,192,256]{3,2,1,0:T(8,128)(2,1)S(1)}, u32[]{:S(2)}, u32[]{:S(2)}) collective-permute-start(bf16[1,2,192,256]{3,2,1,0:T(8,128)(2,1)S(1)} %get-tuple-element.33), channel_id=1, source_target_pairs={{0,16},{16,32},{32,48},{48,64},{64,80},{80,96},{96,112},{112,128},... | collective-permute-start | bytes 589832 | tf_op jit(solution)/shard_map/ppermute | solution.py:24
  19.9 16.7 %collective-permute-start.3 = (bf16[6,1,192,256]{3,2,1,0:T(8,128)(2,1)}, bf16[6,1,192,256]{3,2,1,0:T(8,128)(2,1)}, u32[]{:S(2)}, u32[]{:S(2)}) collective-permute-start(bf16[6,1,192,256]{3,2,1,0:T(8,128)(2,1)} %get-tuple-element.22), channel_id=1, source_target_pairs={{1,0},{2,1},{3,2},{4,3},{5,4},{6,5},{7,6},{8,7},{9,8},{10,9},{11,1... | collective-permute-start | bytes 1769480 | tf_op jit(solution)/shard_map/ppermute | solution.py:26
  21.2 17.1 %collective-permute-start.2 = (bf16[6,1,192,256]{3,2,1,0:T(8,128)(2,1)}, bf16[6,1,192,256]{3,2,1,0:T(8,128)(2,1)}, u32[]{:S(2)}, u32[]{:S(2)}) collective-permute-start(bf16[6,1,192,256]{3,2,1,0:T(8,128)(2,1)} %get-tuple-element.21), channel_id=1, source_target_pairs={{0,1},{1,2},{2,3},{3,4},{4,5},{5,6},{6,7},{7,8},{8,9},{9,10},{10,1... | collective-permute-start | bytes 1769480 | tf_op jit(solution)/shard_map/ppermute | solution.py:24
  41.0 7.9 %slice-start = ((s8[4718592]{0:T(1024)(128)(4,1)}), s8[524288]{0:T(1024)(128)(4,1)S(1)}, s32[]{:S(2)}) async-start(s8[4718592]{0:T(1024)(128)(4,1)} %bitcast.92), calls=%async_computation.2 | async-start | bytes 1048576
  45.9 4.1 slice-start.1
  45.9 4.1 copy-start.4
  52.6 7.3 %collective-permute-start.5 = (bf16[1,2,192,256]{3,2,1,0:T(8,128)(2,1)S(1)}, bf16[1,2,192,256]{3,2,1,0:T(8,128)(2,1)S(1)}, u32[]{:S(2)}, u32[]{:S(2)}) collective-permute-start(bf16[1,2,192,256]{3,2,1,0:T(8,128)(2,1)S(1)} %get-tuple-element.32), channel_id=1, source_target_pairs={{16,0},{32,16},{48,32},{64,48},{80,64},{96,80},{112,96},{128,112},... | collective-permute-start | bytes 589832 | tf_op jit(solution)/shard_map/ppermute | solution.py:26
  54.6 6.4 %collective-permute-start.4 = (bf16[1,2,192,256]{3,2,1,0:T(8,128)(2,1)S(1)}, bf16[1,2,192,256]{3,2,1,0:T(8,128)(2,1)S(1)}, u32[]{:S(2)}, u32[]{:S(2)}) collective-permute-start(bf16[1,2,192,256]{3,2,1,0:T(8,128)(2,1)S(1)} %get-tuple-element.31), channel_id=1, source_target_pairs={{0,16},{16,32},{32,48},{48,64},{64,80},{80,96},{96,112},{112,128},... | collective-permute-start | bytes 589832 | tf_op jit(solution)/shard_map/ppermute | solution.py:24
  61.3 14.9 %collective-permute-start.7 = (bf16[6,1,192,256]{3,2,1,0:T(8,128)(2,1)S(1)}, bf16[6,1,192,256]{3,2,1,0:T(8,128)(2,1)S(1)}, u32[]{:S(2)}, u32[]{:S(2)}) collective-permute-start(bf16[6,1,192,256]{3,2,1,0:T(8,128)(2,1)S(1)} %get-tuple-element.20), channel_id=1, source_target_pairs={{1,0},{2,1},{3,2},{4,3},{5,4},{6,5},{7,6},{8,7},{9,8},{10,9},{11,1... | collective-permute-start | bytes 1769480 | tf_op jit(solution)/shard_map/ppermute | solution.py:26
  62.6 15.4 %collective-permute-start.6 = (bf16[6,1,192,256]{3,2,1,0:T(8,128)(2,1)S(1)}, bf16[6,1,192,256]{3,2,1,0:T(8,128)(2,1)S(1)}, u32[]{:S(2)}, u32[]{:S(2)}) collective-permute-start(bf16[6,1,192,256]{3,2,1,0:T(8,128)(2,1)S(1)} %get-tuple-element.19), channel_id=1, source_target_pairs={{0,1},{1,2},{2,3},{3,4},{4,5},{5,6},{6,7},{7,8},{8,9},{9,10},{10,1... | collective-permute-start | bytes 1769480 | tf_op jit(solution)/shard_map/ppermute | solution.py:24
  79.5 7.9 %slice-start.2 = ((s8[4718592]{0:T(1024)(128)(4,1)}), s8[524288]{0:T(1024)(128)(4,1)S(1)}, s32[]{:S(2)}) async-start(s8[4718592]{0:T(1024)(128)(4,1)} %bitcast.94), calls=%async_computation.4 | async-start | bytes 1048576
  84.4 4.6 %slice-start.3 = ((s8[4718592]{0:T(1024)(128)(4,1)}), s8[4194304]{0:T(1024)(128)(4,1)S(1)}, s32[]{:S(2)}) async-start(s8[4718592]{0:T(1024)(128)(4,1)} %bitcast.94), calls=%async_computation.5 | async-start | bytes 8388608
  84.4 4.6 %copy-start.5 = (f32[4,2,192,256]{3,2,1,0:T(8,128)S(1)}, f32[4,2,192,256]{3,2,1,0:T(8,128)}, u32[]{:S(2)}) copy-start(f32[4,2,192,256]{3,2,1,0:T(8,128)} %param.13) | copy-start | bytes 4718596
  84.5 4.6 %copy-start.11 = (f32[4,2,192,256]{3,2,1,0:T(8,128)S(1)}, f32[4,2,192,256]{3,2,1,0:T(8,128)}, u32[]{:S(2)}) copy-start(f32[4,2,192,256]{3,2,1,0:T(8,128)} %get-tuple-element.36) | copy-start | bytes 4718596
  92.4 12.1 %copy-start.7 = (bf16[4,2,192,256]{3,2,1,0:T(8,128)(2,1)}, bf16[4,2,192,256]{3,2,1,0:T(8,128)(2,1)S(1)}, u32[]{:S(2)}) copy-start(bf16[4,2,192,256]{3,2,1,0:T(8,128)(2,1)S(1)} %get-tuple-element.13) | copy-start | bytes 2359300
  92.4 9.7 %collective-permute-start.9 = (bf16[1,2,192,256]{3,2,1,0:T(8,128)(2,1)S(1)}, bf16[1,2,192,256]{3,2,1,0:T(8,128)(2,1)S(1)}, u32[]{:S(2)}, u32[]{:S(2)}) collective-permute-start(bf16[1,2,192,256]{3,2,1,0:T(8,128)(2,1)S(1)} %get-tuple-element.30), channel_id=1, source_target_pairs={{16,0},{32,16},{48,32},{64,48},{80,64},{96,80},{112,96},{128,112},... | collective-permute-start | bytes 589832 | tf_op jit(solution)/shard_map/ppermute | solution.py:26
  94.3 8.9 %collective-permute-start.8 = (bf16[1,2,192,256]{3,2,1,0:T(8,128)(2,1)S(1)}, bf16[1,2,192,256]{3,2,1,0:T(8,128)(2,1)S(1)}, u32[]{:S(2)}, u32[]{:S(2)}) collective-permute-start(bf16[1,2,192,256]{3,2,1,0:T(8,128)(2,1)S(1)} %get-tuple-element.29), channel_id=1, source_target_pairs={{0,16},{16,32},{32,48},{48,64},{64,80},{80,96},{96,112},{112,128},... | collective-permute-start | bytes 589832 | tf_op jit(solution)/shard_map/ppermute | solution.py:24
  103.4 10.8 %copy-start.14 = (s32[4,2,2]{0,2,1:T(2,128)S(1)}, s32[4,2,2]{0,2,1:T(2,128)}, u32[]{:S(2)}) copy-start(s32[4,2,2]{0,2,1:T(2,128)} %param.17) | copy-start | bytes 196
  104.5 14.3 %copy-start.8 = (bf16[4,2,192,256]{3,2,1,0:T(8,128)(2,1)S(1)}, bf16[4,2,192,256]{3,2,1,0:T(8,128)(2,1)}, u32[]{:S(2)}) copy-start(bf16[4,2,192,256]{3,2,1,0:T(8,128)(2,1)} %copy-done.7) | copy-start | bytes 2359300
  104.5 12.6 %collective-permute-start.11 = (bf16[6,1,192,256]{3,2,1,0:T(8,128)(2,1)}, bf16[6,1,192,256]{3,2,1,0:T(8,128)(2,1)}, u32[]{:S(2)}, u32[]{:S(2)}) collective-permute-start(bf16[6,1,192,256]{3,2,1,0:T(8,128)(2,1)} %get-tuple-element.18), channel_id=1, source_target_pairs={{1,0},{2,1},{3,2},{4,3},{5,4},{6,5},{7,6},{8,7},{9,8},{10,9},{11,1... | collective-permute-start | bytes 1769480 | tf_op jit(solution)/shard_map/ppermute | solution.py:26
  105.9 12.9 %collective-permute-start.10 = (bf16[6,1,192,256]{3,2,1,0:T(8,128)(2,1)}, bf16[6,1,192,256]{3,2,1,0:T(8,128)(2,1)}, u32[]{:S(2)}, u32[]{:S(2)}) collective-permute-start(bf16[6,1,192,256]{3,2,1,0:T(8,128)(2,1)} %get-tuple-element.17), channel_id=1, source_target_pairs={{0,1},{1,2},{2,3},{3,4},{4,5},{5,6},{6,7},{7,8},{8,9},{9,10},{10,1... | collective-permute-start | bytes 1769480 | tf_op jit(solution)/shard_map/ppermute | solution.py:24
  139.4 5.6 %copy-start.15 = (s32[8,3]{0,1:T(4,128)S(1)}, s32[8,3]{0,1:T(4,128)}, u32[]{:S(2)}) copy-start(s32[8,3]{0,1:T(4,128)} %param.19) | copy-start | bytes 292
  144.9 292.0 %all-reduce.5.cloned.1.call-start = ((), (), s32[]{:S(2)}) async-start(), calls=%async_computation.1 | async-start | bytes 786432 | tf_op jit(solution)/shard_map/psum | solution.py:95
  256.1 8.4 %collective-permute-start.13 = (bf16[1,192,256]{2,0,1:T(2,128)(2,1)S(1)}, bf16[1,192,256]{2,0,1:T(2,128)(2,1)S(1)}, u32[]{:S(2)}, u32[]{:S(2)}) collective-permute-start(bf16[1,192,256]{2,0,1:T(2,128)(2,1)S(1)} %get-tuple-element.28), channel_id=1, source_target_pairs={{16,0},{32,16},{48,32},{64,48},{80,64},{96,80},{112,96},{128,112},... | collective-permute-start | bytes 294920 | tf_op jit(solution)/shard_map/ppermute | solution.py:26
  260.0 5.7 %collective-permute-start.12 = (bf16[1,192,256]{2,0,1:T(2,128)(2,1)S(1)}, bf16[1,192,256]{2,0,1:T(2,128)(2,1)S(1)}, u32[]{:S(2)}, u32[]{:S(2)}) collective-permute-start(bf16[1,192,256]{2,0,1:T(2,128)(2,1)S(1)} %get-tuple-element.27), channel_id=1, source_target_pairs={{0,16},{16,32},{32,48},{48,64},{64,80},{80,96},{96,112},{112,128},... | collective-permute-start | bytes 294920 | tf_op jit(solution)/shard_map/ppermute | solution.py:24
  271.1 1.1 copy-start.6
  272.3 11.3 %copy-start.1 = (f32[8,256,192]{1,2,0:T(8,128)}, f32[8,256,192]{1,2,0:T(8,128)S(1)}, u32[]{:S(2)}) copy-start(f32[8,256,192]{1,2,0:T(8,128)S(1)} %convolution_bitcast_fusion.1) | copy-start | bytes 4718596
  273.7 7.7 %collective-permute-start.15 = (bf16[1,192,256]{2,0,1:T(2,128)(2,1)S(1)}, bf16[1,192,256]{2,0,1:T(2,128)(2,1)S(1)}, u32[]{:S(2)}, u32[]{:S(2)}) collective-permute-start(bf16[1,192,256]{2,0,1:T(2,128)(2,1)S(1)} %get-tuple-element.26), channel_id=1, source_target_pairs={{16,0},{32,16},{48,32},{64,48},{80,64},{96,80},{112,96},{128,112},... | collective-permute-start | bytes 294920 | tf_op jit(solution)/shard_map/ppermute | solution.py:26
  275.6 7.0 %collective-permute-start.14 = (bf16[1,192,256]{2,0,1:T(2,128)(2,1)S(1)}, bf16[1,192,256]{2,0,1:T(2,128)(2,1)S(1)}, u32[]{:S(2)}, u32[]{:S(2)}) collective-permute-start(bf16[1,192,256]{2,0,1:T(2,128)(2,1)S(1)} %get-tuple-element.25), channel_id=1, source_target_pairs={{0,16},{16,32},{32,48},{48,64},{64,80},{80,96},{96,112},{112,128},... | collective-permute-start | bytes 294920 | tf_op jit(solution)/shard_map/ppermute | solution.py:24
  290.2 1.4 copy-start.2
  295.1 0.9 copy-start.12
  295.1 10.2 %copy-start.16 = (s32[8,2]{0,1:T(2,128)S(1)}, s32[8,2]{0,1:T(2,128)}, u32[]{:S(2)}) copy-start(s32[8,2]{0,1:T(2,128)} %param.21) | copy-start | bytes 196
  296.2 9.2 %collective-permute-start.17 = (bf16[1,192,256]{2,0,1:T(2,128)(2,1)S(1)}, bf16[1,192,256]{2,0,1:T(2,128)(2,1)}, u32[]{:S(2)}, u32[]{:S(2)}) collective-permute-start(bf16[1,192,256]{2,0,1:T(2,128)(2,1)S(1)} %get-tuple-element.24), channel_id=1, source_target_pairs={{16,0},{32,16},{48,32},{64,48},{80,64},{96,80},{112,96},{128,112},... | collective-permute-start | bytes 294920 | tf_op jit(solution)/shard_map/ppermute | solution.py:26
  298.2 7.3 %collective-permute-start.16 = (bf16[1,192,256]{2,0,1:T(2,128)(2,1)S(1)}, bf16[1,192,256]{2,0,1:T(2,128)(2,1)}, u32[]{:S(2)}, u32[]{:S(2)}) collective-permute-start(bf16[1,192,256]{2,0,1:T(2,128)(2,1)S(1)} %get-tuple-element.23), channel_id=1, source_target_pairs={{0,16},{16,32},{32,48},{48,64},{64,80},{80,96},{96,112},{112,128},... | collective-permute-start | bytes 294920 | tf_op jit(solution)/shard_map/ppermute | solution.py:24
  314.4 1.4 copy-start.3
  314.4 1.9 copy-start.10
  316.3 3.4 copy-start.9
Sparse Core Ops, SparseCore 0:
  145.1 109.3 all-reduce.2
  324.2 112.7 all-reduce.4
where the time goes:
time: 447 us; the launch traced here: 446 us
  waiting for transfers between devices  259 us (58%)
  starting transfers between devices  60.2 us (13%)
  local copies, waits for them, and re-layouts  46.1 us (10%)
  other arithmetic  39.5 us (9%)
  matrix products  26.4 us (6%)
  between operations  14.5 us (3%)
    psum x1, waiting for transfers between devices, middle_level(): lax.psum(local_total.astype(jnp.bfloat16), 'row').astype(jnp.float32)  110 us
    psum x1, waiting for transfers between devices, body(): lax.psum(partial_sum.astype(jnp.bfloat16), 'grid').astype(jnp.float32)  109 us
    ppermute x9, starting transfers between devices, padded(): lax.ppermute(tail, axis, [(i, (i + 1) % count) for i in range(ends)])  39.4 us
    ppermute x9, waiting for transfers between devices, padded(): lax.ppermute(head, axis, [((i + 1) % count, i) for i in range(ends)])  28.5 us
    ppermute x9, starting transfers between devices, padded(): lax.ppermute(head, axis, [((i + 1) % count, i) for i in range(ends)])  20.8 us
    unnamed x48, local copies, waits for them, and re-layouts  16 us
    gather x3, local copies, waits for them, and re-layouts, fine_product(): jnp.take(flattened, position.reshape(-1), axis=0)  14.7 us
    concatenate x9, other arithmetic, padded(): jnp.concatenate([lax.ppermute(tail, axis, [(i, (i + 1) % count) for i in...  11.6 us
  transfers between devices with their start and end apart: 20, of which 18 were waited for; matrix products, arithmetic and copies ran while one was open for 2% of the time, Pallas kernels for 0%

commit v1 on v0

v1 whole, which is shorter than its diff:
```python
import functools

import jax
import jax.numpy as jnp
from jax import lax
from jax.experimental import pallas as pl
from jax.experimental.pallas import tpu as pltpu
from jax.sharding import PartitionSpec as P

MESH = pl.DeviceIdType.MESH
F32 = jnp.float32
BF16 = jnp.bfloat16

C3 = 4
DEG = 3
PARTS = 2

cheb_low = 0.6
cheb_high = 6.0
CENTRE = 0.5 * (cheb_high + cheb_low)
HALF = 0.5 * (cheb_high - cheb_low)


def sweep_factors():
    ratio = CENTRE / HALF
    rho = 1.0 / ratio
    factors = []
    for _ in range(DEG - 1):
        rho_next = 1.0 / (2.0 * ratio - rho)
        factors.append((rho_next * rho, 2.0 * rho_next / HALF))
        rho = rho_next
    return factors


def copy_to(src, dst, send, recv, row, grid):
    return pltpu.make_async_remote_copy(
        src_ref=src, dst_ref=dst, send_sem=send, recv_sem=recv, device_id=(row, grid), device_id_type=MESH
    )


def kernel(
    n_row, n_grid,
    b_hbm, fb_hbm, fc, fp_hbm, ft, mb_hbm, mc, mp_hbm, mt,
    out_f, out_m, out_c,
    res, dirn, itr, fb, fp, mb, mp, halos, pieces, rs_send, rs_recv,
    m_halos, m_res, m_dir, m_itr, ag_send, ag_recv, m_turn, m_out,
    c_pair_send, c_pair_recv, c_z_send, c_z_recv, c_g_send, c_g_recv, c_all, c_turn, c_out,
    in_sem, out_sem, w_sem,
    g_send, g_recv, r_send, r_recv, k_send, k_recv,
    rs_ssem, rs_rsem, mh_send, mh_recv, ag_ssem, ag_rsem,
    cp_ssem, cp_rsem, cz_ssem, cz_rsem, cg_ssem, cg_rsem, ca_ssem, ca_rsem,
):
    r = lax.axis_index("row")
    g = lax.axis_index("grid")
    rx, ry = res.shape[0], res.shape[1]
    bs, loads = res.shape[2], res.shape[3]
    width = loads // PARTS
    lpd = width // n_grid
    LPD = lpd * PARTS
    n_mid = mb.shape[0]
    n_pair = n_row // 2
    core = lax.rem(r, 2)
    mate = r + 1 - 2 * core
    top, bottom = r == 0, r == n_row - 1
    first, last = g == 0, g == n_grid - 1
    half_c = C3 // 2

    for x in range(rx):
        pltpu.make_async_copy(b_hbm.at[x], res.at[x], in_sem.at[x]).start()
    weights = (
        pltpu.make_async_copy(fb_hbm, fb, w_sem.at[0]),
        pltpu.make_async_copy(fp_hbm, fp, w_sem.at[1]),
        pltpu.make_async_copy(mb_hbm, mb, w_sem.at[2]),
        pltpu.make_async_copy(mp_hbm, mp, w_sem.at[3]),
    )
    for w in weights:
        w.start()

    barrier = pltpu.get_barrier_semaphore()

    def greet(row, grid):
        pl.semaphore_signal(barrier, inc=1, device_id=(row, grid), device_id_type=MESH)

    @pl.loop(1, n_grid)
    def _(s):
        greet(r, lax.rem(g + s, n_grid))

    @pl.loop(1, n_pair)
    def _(s):
        greet(lax.rem(r + 2 * s, n_row), g)

    greet(mate, g)
    outer = r - 1 + 2 * core
    has_outer = jnp.logical_and(outer >= 0, outer < n_row)

    @pl.when(has_outer)
    def _():
        greet(outer, g)

    zero = jnp.zeros((bs, width), BF16)

    def clear_row(xi):
        for it in range(DEG):
            for h in range(PARTS):
                for yi in range(ry + 2):
                    halos[it][h][yi, xi] = zero

    def clear_column(yi):
        for it in range(DEG):
            for h in range(PARTS):
                for xi in range(rx + 2):
                    halos[it][h][yi, xi] = zero

    @pl.when(top)
    def _():
        clear_row(0)
        for it in range(DEG):
            m_halos[it][0] = jnp.zeros((LPD, bs), BF16)

    @pl.when(bottom)
    def _():
        clear_row(rx + 1)
        for it in range(DEG):
            m_halos[it][n_mid + 1] = jnp.zeros((LPD, bs), BF16)

    @pl.when(first)
    def _():
        clear_column(0)

    @pl.when(last)
    def _():
        clear_column(ry + 1)

    def send_block(it, h, x, y):
        src = halos[it][h].at[y + 1, x + 1]
        to = g + 2 * y - 1

        @pl.when(jnp.logical_and(to >= 0, to < n_grid))
        def _():
            dst = halos[it][h].at[3 * (1 - y), x + 1]
            copy_to(src, dst, g_send.at[it, h, y, x], g_recv.at[it, h, 1 - y, x], r, to).start()

        @pl.when(jnp.logical_and(x == 0, jnp.logical_not(top)))
        def _():
            dst = halos[it][h].at[y + 1, rx + 1]
            copy_to(src, dst, r_send.at[it, h, 0, y], r_recv.at[it, h, 1, y], r - 1, g).start()

        @pl.when(jnp.logical_and(x == rx - 1, jnp.logical_not(bottom)))
        def _():
            dst = halos[it][h].at[y + 1, 0]
            copy_to(src, dst, r_send.at[it, h, 1, y], r_recv.at[it, h, 0, y], r + 1, g).start()

    def grid_block(it, h, side, x):
        block = halos[it][h].at[3 * side, x + 1]
        return copy_to(block, block, g_send.at[it, h, 1 - side, x], g_recv.at[it, h, side, x], r, g)

    def corner(it, h, up, side):
        src = halos[it][h].at[3 * side, 1 + up * (rx - 1)]
        dst = halos[it][h].at[3 * side, (rx + 1) * (1 - up)]
        return copy_to(src, dst, k_send.at[it, h, up, side], k_recv.at[it, h, 1 - up, side], r - 1 + 2 * up, g)

    def row_block(it, h, up, y):
        block = halos[it][h].at[y + 1, (rx + 1) * up]
        return copy_to(block, block, r_send.at[it, h, up, y], r_recv.at[it, h, up, y], r, g)

    def corner_in(it, h, up, side):
        block = halos[it][h].at[3 * side, (rx + 1) * up]
        return copy_to(block, block, k_send.at[it, h, up, side], k_recv.at[it, h, up, side], r, g)

    sides = ((0, jnp.logical_not(first)), (1, jnp.logical_not(last)))
    ends = ((0, jnp.logical_not(top)), (1, jnp.logical_not(bottom)))

    def forward_corners(it, h):
        for side, there in sides:
            @pl.when(there)
            def _():
                for up, on in ends:
                    grid_block(it, h, side, up * (rx - 1)).wait_recv()

                    @pl.when(on)
                    def _():
                        corner(it, h, up, side).start()

    def wait_halo(it, h):
        for side, there in sides:
            @pl.when(there)
            def _():
                for x in range(1, rx - 1):
                    grid_block(it, h, side, x).wait_recv()
        for up, on in ends:
            @pl.when(on)
            def _():
                for y in range(ry):
                    row_block(it, h, up, y).wait_recv()
                for side, there in sides:
                    @pl.when(there)
                    def _():
                        corner_in(it, h, up, side).wait_recv()

    def order(t):
        return lax.rem(rx - 1 - lax.div(t, ry) + 1, rx), lax.rem(t, ry)

    for x in range(rx):
        pltpu.make_async_copy(b_hbm.at[x], res.at[x], in_sem.at[x]).wait()
    for h in range(PARTS):
        cols = slice(h * width, (h + 1) * width)

        @pl.loop(0, rx * ry)
        def _(t):
            x, y = order(t)
            start = res[x, y, :, cols] * (1.0 / CENTRE)
            halos[0][h][y + 1, x + 1] = start.astype(BF16)
            if h == 0:
                @pl.when(t == 0)
                def _():
                    pl.semaphore_wait(barrier, n_grid - 1 + n_pair + jnp.where(has_outer, 1, 0))
            send_block(0, h, x, y)
            dirn[x, y, :, cols] = start

    weights[0].wait()
    weights[1].wait()
    factors = sweep_factors()
    n_pieces = pieces.shape[0]
    kp = fp.shape[2]

    for it in range(DEG):
        for h in range(PARTS):
            cols = slice(h * width, (h + 1) * width)
            forward_corners(it, h)
            wait_halo(it, h)

            @pl.loop(0, rx * ry)
            def _(t):
                x, y = order(t)
                total = None
                for k in range(fb.shape[2]):
                    c = fc[x, y, k]
                    cx = lax.shift_right_logical(c * 11, 5)
                    picked = halos[it][h][y + c - 3 * cx, x + cx]
                    term = jnp.dot(fb[x, y, k], picked, preferred_element_type=F32)
                    total = term if total is None else total + term
                left = res[x, y, :, cols] - total
                if it < DEG - 1:
                    res[x, y, :, cols] = left
                    alpha, beta = factors[it]
                    old = dirn[x, y, :, cols]
                    new = alpha * old + beta * left
                    halos[it + 1][h][y + 1, x + 1] = new.astype(BF16)
                    send_block(it + 1, h, x, y)
                    if it == 0:
                        dirn[x, y, :, cols] = new
                        itr[x, y, :, cols] = old + new
                    else:
                        itr[x, y, :, cols] = itr[x, y, :, cols] + new
                else:
                    turned = left.astype(BF16).T
                    for k in range(kp):
                        pieces[(x * ry + y) * kp + k] = jnp.dot(turned, fp[x, y, k], preferred_element_type=F32)

            if it == DEG - 2 and h == PARTS - 1:
                pltpu.make_async_copy(itr, out_f, out_sem.at[0]).start()

            if it == DEG - 1:
                def one_share(to):
                    rows = pl.ds(pl.multiple_of(to * lpd, lpd), lpd)
                    sums = [None] * n_mid
                    for p in range(n_pieces):
                        piece = pieces[p, rows, :]
                        target = ft[p // kp // ry, p // kp % ry, p % kp]
                        for m in range(n_mid):
                            part = jnp.where(target == m, piece, 0.0)
                            sums[m] = part if p == 0 else sums[m] + part
                    return jnp.concatenate(sums, axis=0).astype(BF16)

                @pl.loop(1, n_grid)
                def _(s):
                    to = lax.rem(g + s, n_grid)
                    rs_send[h, to] = one_share(to)
                    copy_to(rs_send.at[h, to], rs_recv.at[h, g], rs_ssem.at[h, s], rs_rsem.at[h, g], r, to).start()

                rs_recv[h, g] = one_share(g)

    for h in range(PARTS):
        def take(s, total):
            src = lax.rem(g + n_grid - s, n_grid)
            copy_to(rs_send.at[h, src], rs_recv.at[h, src], rs_ssem.at[h, s], rs_rsem.at[h, src], r, src).wait_recv()
            return total + rs_recv[h, src].astype(F32)

        total = lax.fori_loop(1, n_grid, take, rs_recv[h, g].astype(F32))
        m_res[:, h * lpd:(h + 1) * lpd, :] = total.reshape(n_mid, lpd, bs)

    def send_mid(it):
        @pl.when(jnp.logical_not(top))
        def _():
            copy_to(m_halos[it].at[1], m_halos[it].at[n_mid + 1], mh_send.at[it, 0], mh_recv.at[it, 1], r - 1, g).start()

        @pl.when(jnp.logical_not(bottom))
        def _():
            copy_to(m_halos[it].at[n_mid], m_halos[it].at[0], mh_send.at[it, 1], mh_recv.at[it, 0], r + 1, g).start()

    def mid_block(it, up):
        block = m_halos[it].at[up * (n_mid + 1)]
        return copy_to(block, block, mh_send.at[it, up], mh_recv.at[it, up], r, g)

    start = m_res[...] * (1.0 / CENTRE)
    m_dir[...] = start
    m_halos[0][1:n_mid + 1] = start.astype(BF16)
    send_mid(0)
    weights[2].wait()
    weights[3].wait()

    nt = (((1,), (1,)), ((), ()))
    kp2 = mp.shape[1]
    for it in range(DEG):
        for up, on in ends:
            @pl.when(on)
            def _():
                mid_block(it, up).wait_recv()

        @pl.loop(0, n_mid)
        def _(i):
            total = None
            for k in range(mb.shape[1]):
                picked = m_halos[it][i + mc[i, k]]
                term = lax.dot_general(picked, mb[i, k], nt, preferred_element_type=F32)
                total = term if total is None else total + term
            left = m_res[i] - total
            m_res[i] = left
            if it < DEG - 1:
                alpha, beta = factors[it]
                old = m_dir[i]
                new = alpha * old + beta * left
                m_dir[i] = new
                m_halos[it + 1][i + 1] = new.astype(BF16)
                m_itr[i] = old + new if it == 0 else m_itr[i] + new

        if it < DEG - 1:
            send_mid(it + 1)
        if it == DEG - 2:
            ag_send[...] = m_itr[...].astype(BF16)
            ag_recv[g] = ag_send[...]

            @pl.loop(1, n_grid)
            def _(s):
                to = lax.rem(g + s, n_grid)
                copy_to(ag_send, ag_recv.at[g], ag_ssem.at[s], ag_rsem.at[g], r, to).start()

    sums = [None] * C3
    for i in range(n_mid):
        rounded = m_res[i].astype(BF16)
        for k in range(kp2):
            piece = jnp.dot(rounded, mp[i, k], preferred_element_type=F32)
            for m in range(C3):
                part = jnp.where(mt[i, k] == m, piece, 0.0)
                sums[m] = part if sums[m] is None else sums[m] + part
    low = jnp.stack(sums[:half_c])
    high = jnp.stack(sums[half_c:])
    mine = jnp.where(core == 0, low, high)
    c_pair_send[...] = jnp.where(core == 0, high, low).astype(BF16)
    swap = copy_to(c_pair_send, c_pair_recv, cp_ssem.at[0], cp_rsem.at[0], mate, g)
    swap.start()
    swap.wait()
    mine = mine + c_pair_recv[...].astype(F32)
    c_z_send[...] = mine.astype(BF16)

    @pl.loop(1, n_pair)
    def _(s):
        copy_to(c_z_send, c_z_recv.at[s], cz_ssem.at[s], cz_rsem.at[s], lax.rem(r + 2 * s, n_row), g).start()

    def take_z(s, total):
        copy_to(c_z_send, c_z_recv.at[s], cz_ssem.at[s], cz_rsem.at[s], r, g).wait_recv()
        return total + c_z_recv[s].astype(F32)

    mine = lax.fori_loop(1, n_pair, take_z, mine)
    c_g_send[...] = mine.astype(BF16)

    @pl.loop(1, n_grid)
    def _(s):
        to = lax.rem(g + s, n_grid)
        copy_to(c_g_send, c_g_recv.at[g], cg_ssem.at[s], cg_rsem.at[g], r, to).start()

    c_g_recv[g] = c_g_send[...]
    copy_to(c_g_recv.at[g], c_all.at[g], ca_ssem.at[g], ca_rsem.at[g], mate, g).start()

    @pl.loop(1, n_grid)
    def _(s):
        src = lax.rem(g + n_grid - s, n_grid)
        copy_to(c_g_send, c_g_recv.at[src], cg_ssem.at[s], cg_rsem.at[src], r, g).wait_recv()
        copy_to(c_g_recv.at[src], c_all.at[src], ca_ssem.at[src], ca_rsem.at[src], mate, g).start()

    @pl.loop(1, n_grid)
    def _(s):
        src = lax.rem(g + n_grid - s, n_grid)
        copy_to(ag_send, ag_recv.at[src], ag_ssem.at[s], ag_rsem.at[src], r, g).wait_recv()

    def spread(turn, src, block):
        wide = block.astype(F32)
        for h in range(PARTS):
            rows = pl.ds(pl.multiple_of(h * width + src * lpd, lpd), lpd)
            turn[rows, :] = wide[h * lpd:(h + 1) * lpd]

    @pl.loop(0, n_mid)
    def _(m):
        for src in range(n_grid):
            spread(m_turn, src, ag_recv[src, m])
        m_out[m] = m_turn[...].T

    pltpu.make_async_copy(m_out, out_m, out_sem.at[1]).start()

    @pl.loop(0, n_grid)
    def _(src):
        copy_to(c_g_recv.at[src], c_all.at[src], ca_ssem.at[src], ca_rsem.at[src], mate, g).wait_recv()

    for m in range(half_c):
        for other in range(2):
            source = c_all if other else c_g_recv
            for src in range(n_grid):
                spread(c_turn, src, source[src, m])
            place = m + half_c * (other + core - 2 * other * core)
            c_out[place] = c_turn[...].T

    pltpu.make_async_copy(c_out, out_c, out_sem.at[2]).start()

    for it in range(DEG):
        for h in range(PARTS):
            for y in range(ry):
                to = g + 2 * y - 1

                @pl.when(jnp.logical_and(to >= 0, to < n_grid))
                def _():
                    for x in range(rx):
                        grid_block(it, h, 1 - y, x).wait_send()

            for up, on in ends:
                @pl.when(on)
                def _():
                    for y in range(ry):
                        row_block(it, h, up, y).wait_send()
                    for side, there in sides:
                        @pl.when(there)
                        def _():
                            corner(it, h, up, side).wait_send()
        for up, on in ends:
            @pl.when(on)
            def _():
                mid_block(it, up).wait_send()

    @pl.loop(1, n_grid)
    def _(s):
        to = lax.rem(g + s, n_grid)
        for h in range(PARTS):
            copy_to(rs_send.at[h, to], rs_recv.at[h, g], rs_ssem.at[h, s], rs_rsem.at[h, g], r, to).wait_send()
        copy_to(ag_send, ag_recv.at[g], ag_ssem.at[s], ag_rsem.at[g], r, to).wait_send()
        copy_to(c_g_send, c_g_recv.at[g], cg_ssem.at[s], cg_rsem.at[g], r, to).wait_send()

    @pl.loop(1, n_pair)
    def _(s):
        copy_to(c_z_send, c_z_recv.at[s], cz_ssem.at[s], cz_rsem.at[s], lax.rem(r + 2 * s, n_row), g).wait_send()

    @pl.loop(0, n_grid)
    def _(src):
        copy_to(c_g_recv.at[src], c_all.at[src], ca_ssem.at[src], ca_rsem.at[src], mate, g).wait_send()

    pltpu.make_async_copy(itr, out_f, out_sem.at[0]).wait()
    pltpu.make_async_copy(m_out, out_m, out_sem.at[1]).wait()
    pltpu.make_async_copy(c_out, out_c, out_sem.at[2]).wait()


def body(n_row, n_grid, b, fb, fc, fp, ft, mb, mc, mp, mt):
    rx, ry, bs, loads = b.shape
    width = loads // PARTS
    lpd = width // n_grid
    LPD = lpd * PARTS
    n_mid = mb.shape[0]
    kp = fp.shape[2]
    half_c = C3 // 2
    any_spec = pl.BlockSpec(memory_space=pl.ANY)
    smem = pl.BlockSpec(memory_space=pltpu.SMEM)
    vmem = pltpu.VMEM
    dma = pltpu.SemaphoreType.DMA
    flops = 2 * bs * bs * loads * rx * ry * (fb.shape[2] * DEG + kp)
    return pl.pallas_call(
        functools.partial(kernel, n_row, n_grid),
        out_shape=(
            jax.ShapeDtypeStruct(b.shape, F32),
            jax.ShapeDtypeStruct((n_mid, bs, loads), F32),
            jax.ShapeDtypeStruct((C3, bs, loads), F32),
        ),
        in_specs=[any_spec, any_spec, smem, any_spec, smem, any_spec, smem, any_spec, smem],
        out_specs=(any_spec, any_spec, any_spec),
        scratch_shapes=[
            vmem(b.shape, F32),
            vmem(b.shape, F32),
            vmem(b.shape, F32),
            vmem(fb.shape, BF16),
            vmem(fp.shape, BF16),
            vmem(mb.shape, BF16),
            vmem(mp.shape, BF16),
            [[vmem((ry + 2, rx + 2, bs, width), BF16)] * PARTS] * DEG,
            vmem((rx * ry * kp, width, bs), F32),
            vmem((PARTS, n_grid, n_mid * lpd, bs), BF16),
            vmem((PARTS, n_grid, n_mid * lpd, bs), BF16),
            [vmem((n_mid + 2, LPD, bs), BF16)] * DEG,
            vmem((n_mid, LPD, bs), F32),
            vmem((n_mid, LPD, bs), F32),
            vmem((n_mid, LPD, bs), F32),
            vmem((n_mid, LPD, bs), BF16),
            vmem((n_grid, n_mid, LPD, bs), BF16),
            vmem((loads, bs), F32),
            vmem((n_mid, bs, loads), F32),
            vmem((half_c, LPD, bs), BF16),
            vmem((half_c, LPD, bs), BF16),
            vmem((half_c, LPD, bs), BF16),
            vmem((n_row // 2, half_c, LPD, bs), BF16),
            vmem((half_c, LPD, bs), BF16),
            vmem((n_grid, half_c, LPD, bs), BF16),
            vmem((n_grid, half_c, LPD, bs), BF16),
            vmem((loads, bs), F32),
            vmem((C3, bs, loads), F32),
            dma((rx,)), dma((3,)), dma((4,)),
            dma((DEG, PARTS, 2, rx)), dma((DEG, PARTS, 2, rx)),
            dma((DEG, PARTS, 2, ry)), dma((DEG, PARTS, 2, ry)),
            dma((DEG, PARTS, 2, 2)), dma((DEG, PARTS, 2, 2)),
            dma((PARTS, n_grid)), dma((PARTS, n_grid)),
            dma((DEG, 2)), dma((DEG, 2)),
            dma((n_grid,)), dma((n_grid,)),
            dma((1,)), dma((1,)),
            dma((n_row // 2,)), dma((n_row // 2,)),
            dma((n_grid,)), dma((n_grid,)),
            dma((n_grid,)), dma((n_grid,)),
        ],
        compiler_params=pltpu.CompilerParams(
            collective_id=0, has_side_effects=True, vmem_limit_bytes=56 * 1024 * 1024
        ),
        cost_estimate=pl.CostEstimate(flops=flops, bytes_accessed=13_000_000, transcendentals=0),
    )(b, fb, fc, fp, ft, mb, mc, mp, mt)


def solution(mesh):
    placed = (
        P("row", "grid", None, None),
        P("row", "grid", None, None, None),
        P("row", "grid", None),
        P("row", "grid", None, None, None),
        P("row", "grid", None),
        P("row", None, None, None),
        P("row", None),
        P("row", None, None, None),
        P("row", None),
    )
    return jax.shard_map(
        functools.partial(body, mesh.shape["row"], mesh.shape["grid"]),
        mesh=mesh,
        in_specs=placed,
        out_specs=(P("row", "grid", None, None), P("row", None, None), P()),
        check_vma=False,
    )
```

time: 447 us -> 113 us (0.25)
  waiting for transfers between devices: 259 us -> 0 us
  Pallas kernels: 0 us -> 103 us
  starting transfers between devices: 60.2 us -> 0 us
  other arithmetic: 39.5 us -> 0 us
  local copies, waits for them, and re-layouts: 46.1 us -> 9.38 us
  matrix products: 26.4 us -> 0 us
  between operations: 14.5 us -> 0.65 us
    psum x2 -> x0, waiting for transfers between devices: 219 us -> none  [the longest x1 110 us: middle_level(): lax.psum(local_total.astype(jnp.bfloat16), 'row').astype(jnp.float32)]
    pallas_call x0 -> x1, Pallas kernels: none -> 103 us  [body(): pl.pallas_call(functools.partial(kernel, n_row, n_grid), out_shape=(jax.S...]
    ppermute x18 -> x0, starting transfers between devices: 60.2 us -> none  [the longest x9 39.4 us: padded(): lax.ppermute(tail, axis, [(i, (i + 1) % count) for i in range(ends)])]
    ppermute x18 -> x0, waiting for transfers between devices: 39.9 us -> none  [the longest x9 28.5 us: padded(): lax.ppermute(head, axis, [((i + 1) % count, i) for i in range(ends)])]
    gather x6 -> x0, local copies, waits for them, and re-layouts: 23.7 us -> none  [the longest x3 14.7 us: fine_product(): jnp.take(flattened, position.reshape(-1), axis=0)]
    dot_general x7 -> x0, matrix products: 17.8 us -> none  [the longest x2 9.33 us: scatter_blocks(): jnp.einsum('oz,oay->zay', selection_mask, flattened_parts, precision=lax....]
    select_n x8 -> x0, other arithmetic: 16.9 us -> none  [the longest x4 11.1 us: fine_product(): jnp.take(flattened, position.reshape(-1), axis=0)]
    concatenate x9 -> x0, other arithmetic: 11.6 us -> none  [padded(): jnp.concatenate([lax.ppermute(tail, axis, [(i, (i + 1) % count) for i in...]
  transfers between devices with their start and end apart: 20 -> 0, of which waited for: 18 -> 0; matrix products, arithmetic and copies ran while one was open for 2% -> 0% of each run, Pallas kernels for 0% -> 0%
where the time goes in v1:
time: 113 us
  Pallas kernels  103 us (91%)
  local copies, waits for them, and re-layouts  9.38 us (8%)
    pallas_call x1, Pallas kernels, body(): pl.pallas_call(functools.partial(kernel, n_row, n_grid), out_shape=(jax.S...  103 us
    unnamed x10, local copies, waits for them, and re-layouts  9.38 us

profile of v1, /device:TPU:1, one launch (start us, length us, event | category | flops | bytes accessed | tf_op | source)
XLA Modules:
  0.0 113.2 jit_solution(15257847286470769264)
XLA Ops:
  0.6 1.4 %copy.12.ft = s32[4,2,2]{2,1,0:T(2,128)} copy(s32[4,2,2]{0,2,1:T(2,128)} %param.13) | data formatting | bytes 128 | tf_op args[4]
  2.0 1.3 %copy.13.mc = s32[8,3]{1,0:T(8,128)} copy(s32[8,3]{0,1:T(4,128)} %param.15) | data formatting | bytes 192 | tf_op args[6]
  3.3 1.3 %copy.14.mt = s32[8,2]{1,0:T(8,128)} copy(s32[8,2]{0,1:T(2,128)} %param.17) | data formatting | bytes 128 | tf_op args[8]
  4.7 103.2 %shard_map.112 = (f32[4,2,192,256]{3,2,1,0:T(8,128)}, f32[8,192,256]{2,1,0:T(8,128)}, f32[4,192,256]{2,1,0:T(8,128)}) custom-call(f32[4,2,192,256]{3,2,1,0:T(8,128)} %b_hbm.1, bf16[4,2,6,192,192]{4,3,2,1,0:T(8,128)(2,1)} %fb_hbm.1, s32[4,2,6]{2,1,0:T(2,128)} %fc.1, bf16[4,2,2,192,192]{4,3,2,1,0:T(8,128)(2,1)} %fp_hbm.1, s32[4,2,2]{2,1,0:T(2,128)} %copy.12.ft, ...), custom_call_target="tpu_custom_call" | custom-call | flops 3019898880 | bytes 13000000 | tf_op jit(solution)/shard_map/pallas_call | solution.py:482
  107.9 0.0 copy-start
  107.9 2.8 %copy.18 = f32[4,2,192,256]{3,2,1,0:T(8,128)} copy(f32[4,2,192,256]{3,2,1,0:T(8,128)} %get-tuple-element.6) | data formatting | bytes 3145728
  110.7 0.0 copy-done
  110.7 0.0 copy-start.1
  110.7 1.1 %copy.19 = f32[8,192,256]{2,1,0:T(8,128)} copy(f32[8,192,256]{2,1,0:T(8,128)S(1)} %copy-done) | data formatting | bytes 3145728
  111.8 0.5 copy-done.1
  112.3 0.9 copy.20
Async XLA Ops:
  107.9 2.8 %copy-start = (f32[8,192,256]{2,1,0:T(8,128)S(1)}, f32[8,192,256]{2,1,0:T(8,128)}, u32[]{:S(2)}) copy-start(f32[8,192,256]{2,1,0:T(8,128)} %get-tuple-element.7) | copy-start | bytes 4718596
  110.7 1.7 %copy-start.1 = (f32[4,192,256]{2,1,0:T(8,128)S(1)}, f32[4,192,256]{2,1,0:T(8,128)}, u32[]{:S(2)}) copy-start(f32[4,192,256]{2,1,0:T(8,128)} %get-tuple-element.8) | copy-start | bytes 2359300

commit v2 on v1

--- a/solution.py
+++ b/solution.py
@@ -14,6 +14,8 @@
 C3 = 4
 DEG = 3
 PARTS = 2
+GROUP = 4
+REACH = DEG
 
 cheb_low = 0.6
 cheb_high = 6.0
@@ -43,11 +45,11 @@
     b_hbm, fb_hbm, fc, fp_hbm, ft, mb_hbm, mc, mp_hbm, mt,
     out_f, out_m, out_c,
     res, dirn, itr, fb, fp, mb, mp, halos, pieces, rs_send, rs_recv,
-    m_halos, m_res, m_dir, m_itr, ag_send, ag_recv, m_turn, m_out,
+    m_halos, cols_send, cols_recv, edge_send, m_res, m_dir, m_itr, ag_send, ag_recv, m_turn, m_out,
     c_pair_send, c_pair_recv, c_z_send, c_z_recv, c_g_send, c_g_recv, c_all, c_turn, c_out,
     in_sem, out_sem, w_sem,
     g_send, g_recv, r_send, r_recv, k_send, k_recv,
-    rs_ssem, rs_rsem, mh_send, mh_recv, ag_ssem, ag_rsem,
+    rs_ssem, rs_rsem, mh_send, mh_recv, mb_send, mb_recv, mc_send, mc_recv, ag_ssem, ag_rsem,
     cp_ssem, cp_rsem, cz_ssem, cz_rsem, cg_ssem, cg_rsem, ca_ssem, ca_rsem,
 ):
     r = lax.axis_index("row")
@@ -57,7 +59,8 @@
     width = loads // PARTS
     lpd = width // n_grid
     LPD = lpd * PARTS
-    n_mid = mb.shape[0]
+    n_mid = mb_hbm.shape[0]
+    k2 = mb.shape[1]
     n_pair = n_row // 2
     core = lax.rem(r, 2)
     mate = r + 1 - 2 * core
@@ -70,7 +73,7 @@
     weights = (
         pltpu.make_async_copy(fb_hbm, fb, w_sem.at[0]),
         pltpu.make_async_copy(fp_hbm, fp, w_sem.at[1]),
-        pltpu.make_async_copy(mb_hbm, mb, w_sem.at[2]),
+        pltpu.make_async_copy(mb_hbm, mb.at[pl.ds(REACH - 1, mb_hbm.shape[0])], w_sem.at[2]),
         pltpu.make_async_copy(mp_hbm, mp, w_sem.at[3]),
     )
     for w in weights:
@@ -111,17 +114,23 @@
                 for xi in range(rx + 2):
                     halos[it][h][yi, xi] = zero
 
+    def clear_mid(side):
+        for e in range(REACH):
+            m_res[side * (n_mid + REACH) + e] = jnp.zeros((LPD, bs), F32)
+        cols_recv[side] = jnp.zeros(cols_recv.shape[1:], BF16)
+        for e in range(REACH - 1):
+            for k in range(k2):
+                mb[side * (n_mid + REACH - 1) + e, k] = jnp.zeros((bs, bs), BF16)
+
     @pl.when(top)
     def _():
         clear_row(0)
-        for it in range(DEG):
-            m_halos[it][0] = jnp.zeros((LPD, bs), BF16)
+        clear_mid(0)
 
     @pl.when(bottom)
     def _():
         clear_row(rx + 1)
-        for it in range(DEG):
-            m_halos[it][n_mid + 1] = jnp.zeros((LPD, bs), BF16)
+        clear_mid(1)
 
     @pl.when(first)
     def _():
@@ -198,7 +207,27 @@
                         corner_in(it, h, up, side).wait_recv()
 
     def order(t):
-        return lax.rem(rx - 1 - lax.div(t, ry) + 1, rx), lax.rem(t, ry)
+        return (rx - t // ry) % rx, t % ry
+
+    def mid_matrix(up, q):
+        e, k = q // k2, q % k2
+        src = mb.at[up * n_mid + (1 - up) * (REACH - 1) + e, k]
+        dst = mb.at[(1 - up) * (n_mid + REACH - 1) + e, k]
+        return copy_to(src, dst, mb_send.at[up, q], mb_recv.at[1 - up, q], r - 1 + 2 * up, g)
+
+    def mid_columns(up):
+        return copy_to(cols_send.at[up], cols_recv.at[1 - up], mc_send.at[up], mc_recv.at[1 - up], r - 1 + 2 * up, g)
+
+    def mid_edge(up):
+        src = edge_send.at[up]
+        dst = m_res.at[pl.ds((1 - up) * (n_mid + REACH), REACH)]
+        return copy_to(src, dst, mh_send.at[up], mh_recv.at[1 - up], r - 1 + 2 * up, g)
+
+    for up in range(2):
+        for e in range(REACH - 1):
+            for k in range(k2):
+                own = mc[k, up * (n_mid - REACH + 1) + e].astype(F32)
+                cols_send[up, e, k] = jnp.full((LPD, bs), own, F32).astype(BF16)
 
     for x in range(rx):
         pltpu.make_async_copy(b_hbm.at[x], res.at[x], in_sem.at[x]).wait()
@@ -226,12 +255,21 @@
     for it in range(DEG):
         for h in range(PARTS):
             cols = slice(h * width, (h + 1) * width)
-            forward_corners(it, h)
+            if h == 0:
+                forward_corners(it, h)
             wait_halo(it, h)
-
-            @pl.loop(0, rx * ry)
-            def _(t):
-                x, y = order(t)
+            phase = it * PARTS + h
+            if phase == 0:
+                weights[2].wait()
+            for up, on in ends:
+                @pl.when(on)
+                def _():
+                    if phase == 0:
+                        mid_columns(up).start()
+                    for q in range(phase, (REACH - 1) * k2, DEG * PARTS):
+                        mid_matrix(up, q).start()
+
+            def products(x, y):
                 total = None
                 for k in range(fb.shape[2]):
                     c = fc[x, y, k]
@@ -239,6 +277,9 @@
                     picked = halos[it][h][y + c - 3 * cx, x + cx]
                     term = jnp.dot(fb[x, y, k], picked, preferred_element_type=F32)
                     total = term if total is None else total + term
+                return total
+
+            def update(x, y, total):
                 left = res[x, y, :, cols] - total
                 if it < DEG - 1:
                     res[x, y, :, cols] = left
@@ -246,7 +287,6 @@
                     old = dirn[x, y, :, cols]
                     new = alpha * old + beta * left
                     halos[it + 1][h][y + 1, x + 1] = new.astype(BF16)
-                    send_block(it + 1, h, x, y)
                     if it == 0:
                         dirn[x, y, :, cols] = new
                         itr[x, y, :, cols] = old + new
@@ -257,6 +297,25 @@
                     for k in range(kp):
                         pieces[(x * ry + y) * kp + k] = jnp.dot(turned, fp[x, y, k], preferred_element_type=F32)
 
+            def several(blocks):
+                totals = [products(x, y) for x, y in blocks]
+                for (x, y), total in zip(blocks, totals):
+                    update(x, y, total)
+                if it < DEG - 1:
+                    for x, y in blocks:
+                        send_block(it + 1, h, x, y)
+
+            if GROUP == rx * ry:
+                several([order(t) for t in range(rx * ry)])
+            else:
+                @pl.loop(0, rx * ry // GROUP)
+                def _(t):
+                    several([order(t * GROUP + u) for u in range(GROUP)])
+                    if h + 1 < PARTS:
+                        @pl.when(t == 0)
+                        def _():
+                            forward_corners(it, h + 1)
+
             if it == DEG - 2 and h == PARTS - 1:
                 pltpu.make_async_copy(itr, out_f, out_sem.at[0]).start()
 
@@ -266,19 +325,23 @@
                     sums = [None] * n_mid
                     for p in range(n_pieces):
                         piece = pieces[p, rows, :]
-                        target = ft[p // kp // ry, p // kp % ry, p % kp]
+                        target = ft[p // kp % ry, p % kp, p // kp // ry]
                         for m in range(n_mid):
                             part = jnp.where(target == m, piece, 0.0)
                             sums[m] = part if p == 0 else sums[m] + part
                     return jnp.concatenate(sums, axis=0).astype(BF16)
 
-                @pl.loop(1, n_grid)
-                def _(s):
-                    to = lax.rem(g + s, n_grid)
-                    rs_send[h, to] = one_share(to)
-                    copy_to(rs_send.at[h, to], rs_recv.at[h, g], rs_ssem.at[h, s], rs_rsem.at[h, g], r, to).start()
-
-                rs_recv[h, g] = one_share(g)
+                @pl.loop(0, n_grid // 2)
+                def _(q):
+                    near = [(2 * q + u + 1, lax.rem(g + 2 * q + u + 1, n_grid)) for u in range(2)]
+                    for (_, to), share in zip(near, [one_share(to) for _, to in near]):
+                        rs_send[h, to] = share
+                    for s, to in near:
+                        @pl.when(s < n_grid)
+                        def _():
+                            copy_to(
+                                rs_send.at[h, to], rs_recv.at[h, g], rs_ssem.at[h, s], rs_rsem.at[h, g], r, to
+                            ).start()
 
     for h in range(PARTS):
         def take(s, total):
@@ -286,56 +349,62 @@
             copy_to(rs_send.at[h, src], rs_recv.at[h, src], rs_ssem.at[h, s], rs_rsem.at[h, src], r, src).wait_recv()
             return total + rs_recv[h, src].astype(F32)
 
-        total = lax.fori_loop(1, n_grid, take, rs_recv[h, g].astype(F32))
-        m_res[:, h * lpd:(h + 1) * lpd, :] = total.reshape(n_mid, lpd, bs)
-
-    def send_mid(it):
-        @pl.when(jnp.logical_not(top))
+        total = lax.fori_loop(1, n_grid, take, rs_send[h, g].astype(F32))
+        m_res[REACH:REACH + n_mid, h * lpd:(h + 1) * lpd, :] = total.reshape(n_mid, lpd, bs)
+
+    for up, on in ends:
+        @pl.when(on)
         def _():
-            copy_to(m_halos[it].at[1], m_halos[it].at[n_mid + 1], mh_send.at[it, 0], mh_recv.at[it, 1], r - 1, g).start()
-
-        @pl.when(jnp.logical_not(bottom))
+            edge_send[up] = m_res[up * n_mid + (1 - up) * REACH:up * n_mid + (1 - up) * REACH + REACH]
+            mid_edge(up).start()
+    weights[3].wait()
+    for up, on in ends:
+        @pl.when(on)
         def _():
-            copy_to(m_halos[it].at[n_mid], m_halos[it].at[0], mh_send.at[it, 1], mh_recv.at[it, 0], r + 1, g).start()
-
-    def mid_block(it, up):
-        block = m_halos[it].at[up * (n_mid + 1)]
-        return copy_to(block, block, mh_send.at[it, up], mh_recv.at[it, up], r, g)
+            mid_columns(1 - up).wait_recv()
+            for q in range((REACH - 1) * k2):
+                mid_matrix(1 - up, q).wait_recv()
+            mid_edge(1 - up).wait_recv()
 
     start = m_res[...] * (1.0 / CENTRE)
     m_dir[...] = start
-    m_halos[0][1:n_mid + 1] = start.astype(BF16)
-    send_mid(0)
-    weights[2].wait()
-    weights[3].wait()
+    m_halos[0][...] = start.astype(BF16)
 
     nt = (((1,), (1,)), ((), ()))
     kp2 = mp.shape[1]
     for it in range(DEG):
-        for up, on in ends:
-            @pl.when(on)
-            def _():
-                mid_block(it, up).wait_recv()
-
-        @pl.loop(0, n_mid)
-        def _(i):
+        def mid_products(e):
             total = None
-            for k in range(mb.shape[1]):
-                picked = m_halos[it][i + mc[i, k]]
-                term = lax.dot_general(picked, mb[i, k], nt, preferred_element_type=F32)
+            for k in range(k2):
+                if REACH <= e < REACH + n_mid:
+                    picked = m_halos[it][e - 1 + mc[k, e - REACH]]
+                else:
+                    side = int(e >= REACH)
+                    where = cols_recv[side, e - 1 - side * (n_mid + REACH - 1), k].astype(F32)
+                    near = [m_halos[it][e + d].astype(F32) for d in (-1, 0, 1)]
+                    picked = jnp.where(where == 0.0, near[0], jnp.where(where == 1.0, near[1], near[2])).astype(BF16)
+                term = lax.dot_general(picked, mb[e - 1, k], nt, preferred_element_type=F32)
                 total = term if total is None else total + term
-            left = m_res[i] - total
-            m_res[i] = left
+            return total
+
+        def mid_update(e, total):
+            left = m_res[e] - total
+            m_res[e] = left
             if it < DEG - 1:
                 alpha, beta = factors[it]
-                old = m_dir[i]
+                old = m_dir[e]
                 new = alpha * old + beta * left
-                m_dir[i] = new
-                m_halos[it + 1][i + 1] = new.astype(BF16)
-                m_itr[i] = old + new if it == 0 else m_itr[i] + new
-
-        if it < DEG - 1:
-            send_mid(it + 1)
+                m_dir[e] = new
+                m_halos[it + 1][e] = new.astype(BF16)
+                if REACH <= e < REACH + n_mid:
+                    i = e - REACH
+                    m_itr[i] = old + new if it == 0 else m_itr[i] + new
+
+        rows = range(it + 1, n_mid + 2 * REACH - 1 - it)
+        totals = [mid_products(e) for e in rows]
+        for e, total in zip(rows, totals):
+            mid_update(e, total)
+
         if it == DEG - 2:
             ag_send[...] = m_itr[...].astype(BF16)
             ag_recv[g] = ag_send[...]
@@ -347,11 +416,11 @@
 
     sums = [None] * C3
     for i in range(n_mid):
-        rounded = m_res[i].astype(BF16)
+        rounded = m_res[REACH + i].astype(BF16)
         for k in range(kp2):
             piece = jnp.dot(rounded, mp[i, k], preferred_element_type=F32)
             for m in range(C3):
-                part = jnp.where(mt[i, k] == m, piece, 0.0)
+                part = jnp.where(mt[k, i] == m, piece, 0.0)
                 sums[m] = part if sums[m] is None else sums[m] + part
     low = jnp.stack(sums[:half_c])
     high = jnp.stack(sums[half_c:])
@@ -385,12 +454,6 @@
     @pl.loop(1, n_grid)
     def _(s):
         src = lax.rem(g + n_grid - s, n_grid)
-        copy_to(c_g_send, c_g_recv.at[src], cg_ssem.at[s], cg_rsem.at[src], r, g).wait_recv()
-        copy_to(c_g_recv.at[src], c_all.at[src], ca_ssem.at[src], ca_rsem.at[src], mate, g).start()
-
-    @pl.loop(1, n_grid)
-    def _(s):
-        src = lax.rem(g + n_grid - s, n_grid)
         copy_to(ag_send, ag_recv.at[src], ag_ssem.at[s], ag_rsem.at[src], r, g).wait_recv()
 
     def spread(turn, src, block):
@@ -406,6 +469,12 @@
         m_out[m] = m_turn[...].T
 
     pltpu.make_async_copy(m_out, out_m, out_sem.at[1]).start()
+
+    @pl.loop(1, n_grid)
+    def _(s):
+        src = lax.rem(g + n_grid - s, n_grid)
+        copy_to(c_g_send, c_g_recv.at[src], cg_ssem.at[s], cg_rsem.at[src], r, g).wait_recv()
+        copy_to(c_g_recv.at[src], c_all.at[src], ca_ssem.at[src], ca_rsem.at[src], mate, g).start()
 
     @pl.loop(0, n_grid)
     def _(src):
@@ -420,6 +489,14 @@
             c_out[place] = c_turn[...].T
 
     pltpu.make_async_copy(c_out, out_c, out_sem.at[2]).start()
+
+    for up, on in ends:
+        @pl.when(on)
+        def _():
+            mid_columns(up).wait_send()
+            mid_edge(up).wait_send()
+            for q in range((REACH - 1) * k2):
+                mid_matrix(up, q).wait_send()
 
     for it in range(DEG):
         for h in range(PARTS):
@@ -440,10 +517,6 @@
                         @pl.when(there)
                         def _():
                             corner(it, h, up, side).wait_send()
-        for up, on in ends:
-            @pl.when(on)
-            def _():
-                mid_block(it, up).wait_send()
 
     @pl.loop(1, n_grid)
     def _(s):
@@ -464,6 +537,26 @@
     pltpu.make_async_copy(itr, out_f, out_sem.at[0]).wait()
     pltpu.make_async_copy(m_out, out_m, out_sem.at[1]).wait()
     pltpu.make_async_copy(c_out, out_c, out_sem.at[2]).wait()
+
+
+HAND = 4
+
+
+def hand_over(f, m, c, out_f, out_m, out_c, hold_f, hold_m, hold_c, sem_in, sem_out):
+    arriving, leaving = [], []
+    for n, (src, hold, dst) in enumerate(((f, hold_f, out_f), (m, hold_m, out_m), (c, hold_c, out_c))):
+        part = src.shape[0] // HAND
+        for q in range(HAND):
+            rows = pl.ds(q * part, part)
+            arriving.append(pltpu.make_async_copy(src.at[rows], hold.at[rows], sem_in.at[n, q]))
+            leaving.append(pltpu.make_async_copy(hold.at[rows], dst.at[rows], sem_out.at[n, q]))
+    for copy in arriving:
+        copy.start()
+    for came, goes in zip(arriving, leaving):
+        came.wait()
+        goes.start()
+    for copy in leaving:
+        copy.wait()
 
 
 def body(n_row, n_grid, b, fb, fc, fp, ft, mb, mc, mp, mt):
@@ -479,7 +572,7 @@
     vmem = pltpu.VMEM
     dma = pltpu.SemaphoreType.DMA
     flops = 2 * bs * bs * loads * rx * ry * (fb.shape[2] * DEG + kp)
-    return pl.pallas_call(
+    results = pl.pallas_call(
         functools.partial(kernel, n_row, n_grid),
         out_shape=(
             jax.ShapeDtypeStruct(b.shape, F32),
@@ -494,15 +587,18 @@
             vmem(b.shape, F32),
             vmem(fb.shape, BF16),
             vmem(fp.shape, BF16),
-            vmem(mb.shape, BF16),
+            vmem((n_mid + 2 * REACH - 2,) + mb.shape[1:], BF16),
             vmem(mp.shape, BF16),
             [[vmem((ry + 2, rx + 2, bs, width), BF16)] * PARTS] * DEG,
             vmem((rx * ry * kp, width, bs), F32),
             vmem((PARTS, n_grid, n_mid * lpd, bs), BF16),
             vmem((PARTS, n_grid, n_mid * lpd, bs), BF16),
-            [vmem((n_mid + 2, LPD, bs), BF16)] * DEG,
-            vmem((n_mid, LPD, bs), F32),
-            vmem((n_mid, LPD, bs), F32),
+            [vmem((n_mid + 2 * REACH, LPD, bs), BF16)] * DEG,
+            vmem((2, REACH - 1, mb.shape[1], LPD, bs), BF16),
+            vmem((2, REACH - 1, mb.shape[1], LPD, bs), BF16),
+            vmem((2, REACH, LPD, bs), F32),
+            vmem((n_mid + 2 * REACH, LPD, bs), F32),
+            vmem((n_mid + 2 * REACH, LPD, bs), F32),
             vmem((n_mid, LPD, bs), F32),
             vmem((n_mid, LPD, bs), BF16),
             vmem((n_grid, n_mid, LPD, bs), BF16),
@@ -522,7 +618,9 @@
             dma((DEG, PARTS, 2, ry)), dma((DEG, PARTS, 2, ry)),
             dma((DEG, PARTS, 2, 2)), dma((DEG, PARTS, 2, 2)),
             dma((PARTS, n_grid)), dma((PARTS, n_grid)),
-            dma((DEG, 2)), dma((DEG, 2)),
+            dma((2,)), dma((2,)),
+            dma((2, (REACH - 1) * mb.shape[1])), dma((2, (REACH - 1) * mb.shape[1])),
+            dma((2,)), dma((2,)),
             dma((n_grid,)), dma((n_grid,)),
             dma((1,)), dma((1,)),
             dma((n_row // 2,)), dma((n_row // 2,)),
@@ -533,7 +631,15 @@
             collective_id=0, has_side_effects=True, vmem_limit_bytes=56 * 1024 * 1024
         ),
         cost_estimate=pl.CostEstimate(flops=flops, bytes_accessed=13_000_000, transcendentals=0),
-    )(b, fb, fc, fp, ft, mb, mc, mp, mt)
+    )(b, fb, fc, fp, ft.transpose(1, 2, 0), mb, mc.T, mp, mt.T)
+    return pl.pallas_call(
+        hand_over,
+        out_shape=tuple(jax.ShapeDtypeStruct(o.shape, o.dtype) for o in results),
+        in_specs=[any_spec] * 3,
+        out_specs=(any_spec,) * 3,
+        scratch_shapes=[vmem(o.shape, o.dtype) for o in results] + [dma((3, HAND)), dma((3, HAND))],
+        compiler_params=pltpu.CompilerParams(vmem_limit_bytes=56 * 1024 * 1024),
+    )(*results)
 
 
 def solution(mesh):

time: 113 us -> 91.9 us (0.81)
  the two profiles are of different devices: /device:TPU:1 before, /device:TPU:133 now
where the time goes in v2:
time: 91.9 us; the launch traced here: 91.8 us
  Pallas kernels  91.2 us (99%)
    pallas_call x1, Pallas kernels, body(): pl.pallas_call(functools.partial(kernel, n_row, n_grid), out_shape=(jax.S...  87.8 us
    pallas_call x1, Pallas kernels, body(): pl.pallas_call(hand_over, out_shape=tuple((jax.ShapeDtypeStruct(o.shape,...  3.37 us

profile of v2, /device:TPU:133, one launch (start us, length us, event | category | flops | bytes accessed | tf_op | source)
XLA Modules:
  0.0 91.8 jit_solution(3060079816657174714)
XLA Ops:
  0.6 87.8 %shard_map.112 = (f32[4,2,192,256]{3,2,1,0:T(8,128)}, f32[8,192,256]{2,1,0:T(8,128)}, f32[4,192,256]{2,1,0:T(8,128)}) custom-call(f32[4,2,192,256]{3,2,1,0:T(8,128)} %b_hbm.1, bf16[4,2,6,192,192]{4,3,2,1,0:T(8,128)(2,1)} %fb_hbm.1, s32[4,2,6]{2,1,0:T(2,128)} %fc.1, bf16[4,2,2,192,192]{4,3,2,1,0:T(8,128)(2,1)} %fp_hbm.1, s32[2,2,4]{2,1,0:T(2,128)} %bitcast.3, ...), custom_call_target="tpu_custom_call" | custom-call | flops 3019898880 | bytes 13000000 | tf_op jit(solution)/shard_map/pallas_call | solution.py:575
  88.4 3.4 %shard_map.113 = (f32[4,2,192,256]{3,2,1,0:T(8,128)}, f32[8,192,256]{2,1,0:T(8,128)}, f32[4,192,256]{2,1,0:T(8,128)}) custom-call(f32[4,2,192,256]{3,2,1,0:T(8,128)} %get-tuple-element.6.f, f32[8,192,256]{2,1,0:T(8,128)} %get-tuple-element.7.m, f32[4,192,256]{2,1,0:T(8,128)} %get-tuple-element.8.c), custom_call_target="tpu_custom_call" | custom-call | tf_op jit(solution)/shard_map/pallas_call | solution.py:635

commit v3 on v2

--- a/solution.py
+++ b/solution.py
@@ -329,7 +329,8 @@
                         for m in range(n_mid):
                             part = jnp.where(target == m, piece, 0.0)
                             sums[m] = part if p == 0 else sums[m] + part
-                    return jnp.concatenate(sums, axis=0).astype(BF16)
+                    pairs = [jnp.concatenate(sums[m:m + 2], axis=1) for m in range(0, n_mid, 2)]
+                    return jnp.concatenate(pairs, axis=0).astype(BF16)
 
                 @pl.loop(0, n_grid // 2)
                 def _(q):
@@ -350,7 +351,9 @@
             return total + rs_recv[h, src].astype(F32)
 
         total = lax.fori_loop(1, n_grid, take, rs_send[h, g].astype(F32))
-        m_res[REACH:REACH + n_mid, h * lpd:(h + 1) * lpd, :] = total.reshape(n_mid, lpd, bs)
+        for m in range(n_mid):
+            half = total[m // 2 * lpd:(m // 2 + 1) * lpd, m % 2 * bs:(m % 2 + 1) * bs]
+            m_res[REACH + m, h * lpd:(h + 1) * lpd, :] = half
 
     for up, on in ends:
         @pl.when(on)
@@ -406,7 +409,8 @@
             mid_update(e, total)
 
         if it == DEG - 2:
-            ag_send[...] = m_itr[...].astype(BF16)
+            for q in range(n_mid // 2):
+                ag_send[q] = jnp.concatenate([m_itr[2 * q], m_itr[2 * q + 1]], axis=1).astype(BF16)
             ag_recv[g] = ag_send[...]
 
             @pl.loop(1, n_grid)
@@ -462,11 +466,13 @@
             rows = pl.ds(pl.multiple_of(h * width + src * lpd, lpd), lpd)
             turn[rows, :] = wide[h * lpd:(h + 1) * lpd]
 
-    @pl.loop(0, n_mid)
-    def _(m):
+    @pl.loop(0, n_mid // 2)
+    def _(q):
         for src in range(n_grid):
-            spread(m_turn, src, ag_recv[src, m])
-        m_out[m] = m_turn[...].T
+            spread(m_turn, src, ag_recv[src, q])
+        turned = m_turn[...].T
+        m_out[2 * q] = turned[:bs]
+        m_out[2 * q + 1] = turned[bs:]
 
     pltpu.make_async_copy(m_out, out_m, out_sem.at[1]).start()
 
@@ -591,8 +597,8 @@
             vmem(mp.shape, BF16),
             [[vmem((ry + 2, rx + 2, bs, width), BF16)] * PARTS] * DEG,
             vmem((rx * ry * kp, width, bs), F32),
-            vmem((PARTS, n_grid, n_mid * lpd, bs), BF16),
-            vmem((PARTS, n_grid, n_mid * lpd, bs), BF16),
+            vmem((PARTS, n_grid, n_mid // 2 * lpd, 2 * bs), BF16),
+            vmem((PARTS, n_grid, n_mid // 2 * lpd, 2 * bs), BF16),
             [vmem((n_mid + 2 * REACH, LPD, bs), BF16)] * DEG,
             vmem((2, REACH - 1, mb.shape[1], LPD, bs), BF16),
             vmem((2, REACH - 1, mb.shape[1], LPD, bs), BF16),
@@ -600,9 +606,9 @@
             vmem((n_mid + 2 * REACH, LPD, bs), F32),
             vmem((n_mid + 2 * REACH, LPD, bs), F32),
             vmem((n_mid, LPD, bs), F32),
-            vmem((n_mid, LPD, bs), BF16),
-            vmem((n_grid, n_mid, LPD, bs), BF16),
-            vmem((loads, bs), F32),
+            vmem((n_mid // 2, LPD, 2 * bs), BF16),
+            vmem((n_grid, n_mid // 2, LPD, 2 * bs), BF16),
+            vmem((loads, 2 * bs), F32),
             vmem((n_mid, bs, loads), F32),
             vmem((half_c, LPD, bs), BF16),
             vmem((half_c, LPD, bs), BF16),

time: 91.9 us -> 89 us (0.968)
  the two profiles are of different devices: /device:TPU:133 before, /device:TPU:1 now
where the time goes in v3:
time: 89 us; the launch traced here: 88.8 us
  Pallas kernels  88.2 us (99%)
    pallas_call x1, Pallas kernels, body(): pl.pallas_call(functools.partial(kernel, n_row, n_grid), out_shape=(jax.S...  84.8 us
    pallas_call x1, Pallas kernels, body(): pl.pallas_call(hand_over, out_shape=tuple((jax.ShapeDtypeStruct(o.shape,...  3.37 us

profile of v3, /device:TPU:1, one launch (start us, length us, event | category | flops | bytes accessed | tf_op | source)
XLA Modules:
  0.0 88.8 jit_solution(14064118831229799833)
XLA Ops:
  0.6 84.8 %shard_map.112 = (f32[4,2,192,256]{3,2,1,0:T(8,128)}, f32[8,192,256]{2,1,0:T(8,128)}, f32[4,192,256]{2,1,0:T(8,128)}) custom-call(f32[4,2,192,256]{3,2,1,0:T(8,128)} %b_hbm.1, bf16[4,2,6,192,192]{4,3,2,1,0:T(8,128)(2,1)} %fb_hbm.1, s32[4,2,6]{2,1,0:T(2,128)} %fc.1, bf16[4,2,2,192,192]{4,3,2,1,0:T(8,128)(2,1)} %fp_hbm.1, s32[2,2,4]{2,1,0:T(2,128)} %bitcast.3, ...), custom_call_target="tpu_custom_call" | custom-call | flops 3019898880 | bytes 13000000 | tf_op jit(solution)/shard_map/pallas_call | solution.py:581
  85.5 3.4 %shard_map.113 = (f32[4,2,192,256]{3,2,1,0:T(8,128)}, f32[8,192,256]{2,1,0:T(8,128)}, f32[4,192,256]{2,1,0:T(8,128)}) custom-call(f32[4,2,192,256]{3,2,1,0:T(8,128)} %get-tuple-element.6.f, f32[8,192,256]{2,1,0:T(8,128)} %get-tuple-element.7.m, f32[4,192,256]{2,1,0:T(8,128)} %get-tuple-element.8.c), custom_call_target="tpu_custom_call" | custom-call | tf_op jit(solution)/shard_map/pallas_call | solution.py:641

commit v4 on v3

--- a/solution.py
+++ b/solution.py
@@ -426,8 +426,8 @@
             for m in range(C3):
                 part = jnp.where(mt[k, i] == m, piece, 0.0)
                 sums[m] = part if sums[m] is None else sums[m] + part
-    low = jnp.stack(sums[:half_c])
-    high = jnp.stack(sums[half_c:])
+    low = jnp.concatenate(sums[:half_c], axis=1)
+    high = jnp.concatenate(sums[half_c:], axis=1)
     mine = jnp.where(core == 0, low, high)
     c_pair_send[...] = jnp.where(core == 0, high, low).astype(BF16)
     swap = copy_to(c_pair_send, c_pair_recv, cp_ssem.at[0], cp_rsem.at[0], mate, g)
@@ -486,13 +486,14 @@
     def _(src):
         copy_to(c_g_recv.at[src], c_all.at[src], ca_ssem.at[src], ca_rsem.at[src], mate, g).wait_recv()
 
-    for m in range(half_c):
-        for other in range(2):
-            source = c_all if other else c_g_recv
-            for src in range(n_grid):
-                spread(c_turn, src, source[src, m])
+    for other in range(2):
+        source = c_all if other else c_g_recv
+        for src in range(n_grid):
+            spread(c_turn, src, source[src])
+        turned = c_turn[...].T
+        for m in range(half_c):
             place = m + half_c * (other + core - 2 * other * core)
-            c_out[place] = c_turn[...].T
+            c_out[place] = turned[m * bs:(m + 1) * bs]
 
     pltpu.make_async_copy(c_out, out_c, out_sem.at[2]).start()
 
@@ -610,14 +611,14 @@
             vmem((n_grid, n_mid // 2, LPD, 2 * bs), BF16),
             vmem((loads, 2 * bs), F32),
             vmem((n_mid, bs, loads), F32),
-            vmem((half_c, LPD, bs), BF16),
-            vmem((half_c, LPD, bs), BF16),
-            vmem((half_c, LPD, bs), BF16),
-            vmem((n_row // 2, half_c, LPD, bs), BF16),
-            vmem((half_c, LPD, bs), BF16),
-            vmem((n_grid, half_c, LPD, bs), BF16),
-            vmem((n_grid, half_c, LPD, bs), BF16),
-            vmem((loads, bs), F32),
+            vmem((LPD, half_c * bs), BF16),
+            vmem((LPD, half_c * bs), BF16),
+            vmem((LPD, half_c * bs), BF16),
+            vmem((n_row // 2, LPD, half_c * bs), BF16),
+            vmem((LPD, half_c * bs), BF16),
+            vmem((n_grid, LPD, half_c * bs), BF16),
+            vmem((n_grid, LPD, half_c * bs), BF16),
+            vmem((loads, half_c * bs), F32),
             vmem((C3, bs, loads), F32),
             dma((rx,)), dma((3,)), dma((4,)),
             dma((DEG, PARTS, 2, rx)), dma((DEG, PARTS, 2, rx)),

time: 89 us -> 87.4 us (0.982)
  Pallas kernels: 88.2 us -> 86.6 us
    pallas_call x1, Pallas kernels: 84.8 us -> 83.3 us  [body(): pl.pallas_call(functools.partial(kernel, n_row, n_grid), out_shape=(jax.S...]
where the time goes in v4:
time: 87.4 us; the launch traced here: 87.3 us
  Pallas kernels  86.6 us (99%)
    pallas_call x1, Pallas kernels, body(): pl.pallas_call(functools.partial(kernel, n_row, n_grid), out_shape=(jax.S...  83.3 us
    pallas_call x1, Pallas kernels, body(): pl.pallas_call(hand_over, out_shape=tuple((jax.ShapeDtypeStruct(o.shape,...  3.37 us

profile of v4, /device:TPU:1, one launch (start us, length us, event | category | flops | bytes accessed | tf_op | source)
XLA Modules:
  0.0 87.3 jit_solution(14713336251566120393)
XLA Ops:
  0.6 83.3 %shard_map.112 = (f32[4,2,192,256]{3,2,1,0:T(8,128)}, f32[8,192,256]{2,1,0:T(8,128)}, f32[4,192,256]{2,1,0:T(8,128)}) custom-call(f32[4,2,192,256]{3,2,1,0:T(8,128)} %b_hbm.1, bf16[4,2,6,192,192]{4,3,2,1,0:T(8,128)(2,1)} %fb_hbm.1, s32[4,2,6]{2,1,0:T(2,128)} %fc.1, bf16[4,2,2,192,192]{4,3,2,1,0:T(8,128)(2,1)} %fp_hbm.1, s32[2,2,4]{2,1,0:T(2,128)} %bitcast.3, ...), custom_call_target="tpu_custom_call" | custom-call | flops 3019898880 | bytes 13000000 | tf_op jit(solution)/shard_map/pallas_call | solution.py:582
  83.9 3.4 %shard_map.113 = (f32[4,2,192,256]{3,2,1,0:T(8,128)}, f32[8,192,256]{2,1,0:T(8,128)}, f32[4,192,256]{2,1,0:T(8,128)}) custom-call(f32[4,2,192,256]{3,2,1,0:T(8,128)} %get-tuple-element.6.f, f32[8,192,256]{2,1,0:T(8,128)} %get-tuple-element.7.m, f32[4,192,256]{2,1,0:T(8,128)} %get-tuple-element.8.c), custom_call_target="tpu_custom_call" | custom-call | tf_op jit(solution)/shard_map/pallas_call | solution.py:642
